TPU v7x, 32 devices: a whole 2x2x4 slice. The times are simulated.
32 devices in a mesh: dp: 8 (over z, y), row: 2 (over core), col: 2 (over x).
Axes of the slice: x: 2, y: 2, z: 4, core: 2. Of those that a mesh axis runs over, the one named last changes fastest.
Arguments:
- block_input: bfloat16 [4096, 2560], P(('dp', 'col')), may hold values from -6 to 6
- cotangent: bfloat16 [4096, 2560], P(('dp', 'col'), 'row'), may hold values from -6 to 6
- seq_lengths: int32 [32], replicated, may hold values from 16 to 128, as said below
- seq_owner: int32 [32], replicated, may hold values from 0 to 15, as said below
- norm_gain: bfloat16 [2560], P('row'), may hold values from 0.5 to 1.5
- proj_zx: bfloat16 [2560, 2, 5120], P('row', None, 'col'), may hold values from -0.125 to 0.125
- proj_bc: bfloat16 [2560, 256], P('row'), may hold values from -0.125 to 0.125
- proj_dt: bfloat16 [2560, 80], P('row', 'col'), may hold values from -0.125 to 0.125
- proj_out: bfloat16 [5120, 2560], P('col', 'row'), may hold values from -0.078125 to 0.078125
- inner_kernel: float32 [4, 5120], P(None, 'col'), may hold values from -3 to 3
- inner_offset: float32 [5120], P('col'), may hold values from -1.5 to 1.5
- shared_kernel: float32 [4, 256], replicated, may hold values from -3 to 3
- shared_offset: float32 [256], replicated, may hold values from -1.5 to 1.5
- decay_log: float32 [80], P('col'), may hold values from 0 to 2.77
- step_bias: float32 [80], P('col'), may hold values from -6 to -2
- skip_gain: float32 [80], P('col'), may hold values from 0.5 to 1.5
- output_gain: bfloat16 [5120], P('col'), may hold values from 0.5 to 1.5
Outputs:
- block_output: bfloat16 [4096, 2560], P(('dp', 'col'), 'row')
- input_grad: float32 [4096, 2560], P(('dp', 'col'), 'row')
- grad_norm: float32 [2560], P('row')
- grad_inproj: float32 [2560, 2, 5120], P('row', None, 'col')
- grad_shared: float32 [2560, 256], P('row')
- grad_steps: float32 [2560, 80], P('row', 'col')
- grad_outproj: float32 [5120, 2560], P('col', 'row')
- grad_kernel: float32 [4, 5120], P(None, 'col')
- grad_offset: float32 [5120], P('col')
- grad_skernel: float32 [4, 256], replicated
- grad_soffset: float32 [256], replicated
- grad_decay: float32 [80], P('col')
- grad_stepbias: float32 [80], P('col')
- grad_skip: float32 [80], P('col')
- grad_ogain: float32 [5120], P('col')
Inputs may be any that keep to these rules, and one draw needn't show every extreme that they name: `seq_lengths`: the lengths of the 2 sequences of one bucket sum to at most 256; in every draw some bucket holds 2 sequences of exactly 128 rows, so that its sum is 256. `seq_owner`: every bucket owns exactly 2 sequences.
All inputs are finite; a program needn't handle non-finite values.
Results may differ from a plain program's by a relative error of at most 0.0079.
The roundings to bfloat16 on the way count: a program that leaves them out, or rounds other values in their place, can miss the bound.
Values may be sent and summed in bfloat16 or wider, within the bound.
A program may use at most 256 MiB of HBM per device.

v0:
```python
import jax
import jax.numpy as jnp
from jax import lax
from jax.sharding import PartitionSpec as P

D = 2560
DI = 5120
SCAN_BLOCK = 256
CAP = 256
EPSILON = 1e-05
PRECISE = lax.Precision.HIGHEST


def layout(seq_lengths, seq_owner, bucket, capacity):
    owned = seq_owner == bucket
    owned_len = jnp.where(owned, seq_lengths, 0)
    starts = jnp.cumsum(owned_len) - owned_len
    places = jnp.arange(capacity, dtype=jnp.int32)[:, None]
    ends = starts + seq_lengths
    inside = owned[None, :] & (places >= starts[None, :]) & (places < ends[None, :])
    live_rows = jnp.any(inside, axis=1)
    seq_index = jnp.arange(seq_lengths.shape[0], dtype=jnp.int32)
    seq_ids = jnp.sum(jnp.where(inside, seq_index[None, :], 0), axis=1)
    seq_ids = jnp.where(live_rows, seq_ids, -1)
    return (seq_ids, live_rows.astype(jnp.float32))


def convolve(channels, kernel, offset, seq_ids, live_rows):
    tap_count = kernel.shape[0]
    summed_in = offset[None, :] + kernel[tap_count - 1][None, :] * channels
    for lag_steps in range(1, tap_count):
        lagged = jnp.concatenate(
            [jnp.zeros((lag_steps, channels.shape[1]), jnp.float32), channels[:-lag_steps]], axis=0
        )
        prior_ids = jnp.concatenate([jnp.full((lag_steps,), -1, jnp.int32), seq_ids[:-lag_steps]])
        same_seq = jnp.where((prior_ids == seq_ids) & (live_rows > 0), 1.0, 0.0).astype(jnp.float32)
        summed_in = (
            summed_in + kernel[tap_count - 1 - lag_steps][None, :] * lagged * same_seq[:, None]
        )
    return summed_in


def scan_blocks(
    values, inputs_b, inputs_c, step_sizes, decay_rate, skip_gain, seq_ids, live_rows, block_len
):
    rows_all, head_count, head_dim = values.shape
    state_size = inputs_b.shape[1]
    block_count = rows_all // block_len
    lower = jnp.arange(block_len)[:, None] >= jnp.arange(block_len)[None, :]

    def one_block(carried_in, block_item):
        memory, last_id = carried_in
        vals, bmat, cmat, sizes, rates, ids_here, live_here = block_item
        cumulated = jnp.cumsum(rates, axis=0)
        pair_live = (
            (ids_here[:, None] == ids_here[None, :])
            & (live_here[:, None] > 0)
            & (live_here[None, :] > 0)
            & lower
        )
        pair_mask = pair_live.astype(jnp.float32)
        scores = jnp.dot(cmat, bmat.T, precision=PRECISE)
        gap = jnp.where(pair_live[:, :, None], cumulated[:, None, :] - cumulated[None, :, :], 0.0)
        weights = jnp.exp(gap) * (pair_mask * scores)[:, :, None] * sizes[None, :, :]
        within = jnp.einsum("tsh,shp->thp", weights, vals, precision=PRECISE)
        carried = jnp.where((ids_here == last_id) & (live_here > 0), 1.0, 0.0).astype(jnp.float32)
        recalled = jnp.einsum("hpn,tn->thp", memory, cmat, precision=PRECISE)
        recalled = recalled * (jnp.exp(cumulated) * carried[:, None])[:, :, None]
        mixed_out = (within + recalled + skip_gain[None, :, None] * vals) * live_here[:, None, None]
        factor = jnp.exp(cumulated[-1][None, :] - cumulated) * pair_mask[-1][:, None] * sizes
        fresh_state = jnp.einsum("sh,shp,sn->hpn", factor, vals, bmat, precision=PRECISE)
        continues = jnp.where((ids_here[-1] == last_id) & (live_here[-1] > 0), 1.0, 0.0).astype(
            jnp.float32
        )
        memory = continues * jnp.exp(cumulated[-1])[:, None, None] * memory + fresh_state
        return ((memory, ids_here[-1]), mixed_out)

    items = (
        values.reshape(block_count, block_len, head_count, head_dim),
        inputs_b.reshape(block_count, block_len, state_size),
        inputs_c.reshape(block_count, block_len, state_size),
        step_sizes.reshape(block_count, block_len, head_count),
        decay_rate.reshape(block_count, block_len, head_count),
        seq_ids.reshape(block_count, block_len),
        live_rows.reshape(block_count, block_len),
    )
    start_state = (jnp.zeros((head_count, head_dim, state_size), jnp.float32), jnp.int32(-2))
    _, outputs = lax.scan(jax.checkpoint(one_block), start_state, items)
    return outputs.reshape(rows_all, head_count * head_dim)


def mixer_local(
    mixer_in,
    inner_kernel,
    inner_offset,
    shared_kernel,
    shared_offset,
    decay_log,
    step_bias,
    skip_gain,
    seq_ids,
    live_rows,
    block_len,
):
    inner_size = inner_kernel.shape[1]
    state_size = shared_kernel.shape[1] // 2
    head_count = decay_log.shape[0]
    gate_in = mixer_in[:, :inner_size]
    conv_in = mixer_in[:, inner_size : 2 * inner_size]
    shared_in = mixer_in[:, 2 * inner_size : 2 * inner_size + 2 * state_size]
    step_raw = mixer_in[:, 2 * inner_size + 2 * state_size :]
    mixed_x = jax.nn.silu(convolve(conv_in, inner_kernel, inner_offset, seq_ids, live_rows))
    mixed_bc = jax.nn.silu(convolve(shared_in, shared_kernel, shared_offset, seq_ids, live_rows))
    step_sizes = jax.nn.softplus(step_raw + step_bias[None, :])
    decay_rate = step_sizes * (-jnp.exp(decay_log))[None, :]
    values = mixed_x.reshape(mixed_x.shape[0], head_count, inner_size // head_count)
    ssm_out = scan_blocks(
        values,
        mixed_bc[:, :state_size],
        mixed_bc[:, state_size:],
        step_sizes,
        decay_rate,
        skip_gain,
        seq_ids,
        live_rows,
        block_len,
    )
    return ssm_out * jax.nn.silu(gate_in)


def per_device(
    block_input,
    cotangent,
    seq_lengths,
    seq_owner,
    norm_gain,
    proj_zx,
    proj_bc,
    proj_dt,
    proj_out,
    inner_kernel,
    inner_offset,
    shared_kernel,
    shared_offset,
    decay_log,
    step_bias,
    skip_gain,
    output_gain,
):
    row_count = lax.axis_size("row")
    col_count = lax.axis_size("col")
    row_index = lax.axis_index("row")
    col_index = lax.axis_index("col")
    data_index = lax.axis_index("dp")
    width_part = norm_gain.shape[0]
    inner_size = proj_zx.shape[2]
    state_size = proj_bc.shape[1] // 2
    tap_count = inner_kernel.shape[0]
    capacity = CAP
    bucket = data_index * row_count + row_index
    seq_ids, live_rows = layout(seq_lengths, seq_owner, bucket, capacity)
    rscale = lax.rsqrt(
        jnp.mean(jnp.square(block_input.astype(jnp.float32)), axis=1, keepdims=True) + EPSILON
    )
    own_cols = lax.dynamic_slice_in_dim(block_input, row_index * width_part, width_part, 1).astype(
        jnp.float32
    )
    normalized = own_cols * rscale
    gain_f = norm_gain.astype(jnp.float32)
    normed = (normalized * gain_f[None, :]).astype(jnp.bfloat16)
    normed_all = lax.all_gather(normed, "col", axis=0, tiled=True)
    weight_in = jnp.concatenate([proj_zx[:, 0, :], proj_zx[:, 1, :], proj_bc, proj_dt], axis=1)
    row_piece = normed_all
    mixer_in = lax.psum_scatter(
        jnp.dot(row_piece, weight_in, preferred_element_type=jnp.float32),
        "row",
        scatter_dimension=0,
        tiled=True,
    )

    def local_piece(
        mixer_value, kernel_a, offset_a, kernel_b, offset_b, decay_value, bias_value, skip_value
    ):
        return mixer_local(
            mixer_value,
            kernel_a,
            offset_a,
            kernel_b,
            offset_b,
            decay_value,
            bias_value,
            skip_value,
            seq_ids,
            live_rows,
            SCAN_BLOCK,
        )

    gated_rows, pull_back = jax.vjp(
        local_piece,
        mixer_in,
        inner_kernel,
        inner_offset,
        shared_kernel,
        shared_offset,
        decay_log,
        step_bias,
        skip_gain,
    )
    square_sum = lax.psum(jnp.sum(gated_rows * gated_rows, axis=1), "col")
    rnorm = lax.rsqrt(square_sum / DI + EPSILON)[:, None]
    out_gain = output_gain.astype(jnp.float32)
    branch = (gated_rows * rnorm * out_gain[None, :]).astype(jnp.bfloat16)
    branch_all = lax.all_gather(branch, "row", axis=0, tiled=True)
    row_piece = branch_all
    branch_out = lax.psum_scatter(
        jnp.dot(row_piece, proj_out, preferred_element_type=jnp.float32),
        "col",
        scatter_dimension=0,
        tiled=True,
    )
    block_output = (own_cols + branch_out).astype(jnp.bfloat16)
    cot_all = lax.all_gather(cotangent, "col", axis=0, tiled=True)
    row_piece = cot_all
    branch_grad = lax.psum_scatter(
        lax.dot_general(
            row_piece, proj_out, (((1,), (1,)), ((), ())), preferred_element_type=jnp.float32
        ),
        "row",
        scatter_dimension=0,
        tiled=True,
    )
    outproj_part = lax.dot_general(
        branch_all, cot_all, (((0,), (0,)), ((), ())), preferred_element_type=jnp.float32
    )
    outproj_total = outproj_part
    scaled_grad = branch_grad * out_gain[None, :]
    cross_sum = lax.psum(jnp.sum(scaled_grad * gated_rows, axis=1), "col")
    gated_grad = rnorm * scaled_grad - gated_rows * rnorm**3 * (cross_sum / DI)[:, None]
    ogain_part = jnp.sum(branch_grad * gated_rows * rnorm, axis=0)
    local_grads = pull_back(gated_grad)
    mixer_grad = local_grads[0].astype(jnp.bfloat16)
    mixer_all = lax.all_gather(mixer_grad, "row", axis=0, tiled=True)
    row_piece = mixer_all
    normed_grad = lax.psum_scatter(
        lax.dot_general(
            row_piece, weight_in, (((1,), (1,)), ((), ())), preferred_element_type=jnp.float32
        ),
        "col",
        scatter_dimension=0,
        tiled=True,
    )
    weight_grad = lax.dot_general(
        normed_all, mixer_all, (((0,), (0,)), ((), ())), preferred_element_type=jnp.float32
    )
    inproj_part = jnp.stack(
        [weight_grad[:, :inner_size], weight_grad[:, inner_size : 2 * inner_size]], axis=1
    )
    shared_part = weight_grad[:, 2 * inner_size : 2 * inner_size + 2 * state_size]
    steps_part = weight_grad[:, 2 * inner_size + 2 * state_size :]
    scaled_in = normed_grad * gain_f[None, :]
    norm_part = jnp.sum(normed_grad * normalized, axis=0)
    row_stat = lax.psum(jnp.sum(scaled_in * normalized, axis=1), "row")
    input_grad = cotangent.astype(jnp.float32) + rscale * (
        scaled_in - normalized * (row_stat / D)[:, None]
    )
    inproj_total, steps_total, outproj_total = lax.psum(
        (inproj_part, steps_part, outproj_total), "dp"
    )
    row_hot = (jnp.arange(row_count) == row_index).astype(jnp.float32)
    col_hot = (jnp.arange(col_count) == col_index).astype(jnp.float32)
    gain_slot = row_hot[:, None] * norm_part[None, :]
    shared_slot = row_hot[:, None, None] * shared_part[None, :, :]
    head_stack = jnp.stack([local_grads[5], local_grads[6], local_grads[7]], axis=0)
    head_slot = col_hot[None, :, None] * head_stack[:, None, :]
    chan_stack = jnp.concatenate(
        [local_grads[1], local_grads[2][None, :], ogain_part[None, :]], axis=0
    )
    chan_slot = col_hot[None, :, None] * chan_stack[:, None, :]
    shared_stack = jnp.concatenate([local_grads[3], local_grads[4][None, :]], axis=0)
    summed = lax.psum(
        (gain_slot, shared_slot, head_slot, chan_slot, shared_stack), ("dp", "row", "col")
    )
    gain_total = lax.dynamic_index_in_dim(summed[0], row_index, 0, keepdims=False)
    shared_total = lax.dynamic_index_in_dim(summed[1], row_index, 0, keepdims=False)
    head_total = lax.dynamic_index_in_dim(summed[2], col_index, 1, keepdims=False)
    chan_total = lax.dynamic_index_in_dim(summed[3], col_index, 1, keepdims=False)
    stack_total = summed[4]
    return (
        block_output,
        input_grad,
        gain_total,
        inproj_total,
        shared_total,
        steps_total,
        outproj_total,
        chan_total[:tap_count],
        chan_total[tap_count],
        stack_total[:tap_count],
        stack_total[tap_count],
        head_total[0],
        head_total[1],
        head_total[2],
        chan_total[tap_count + 1],
    )


def solution(mesh):
    return jax.shard_map(
        per_device,
        mesh=mesh,
        in_specs=(
            P(("dp", "col"), None),
            P(("dp", "col"), "row"),
            P(),
            P(),
            P("row"),
            P("row", None, "col"),
            P("row", None),
            P("row", "col"),
            P("col", "row"),
            P(None, "col"),
            P("col"),
            P(),
            P(),
            P("col"),
            P("col"),
            P("col"),
            P("col"),
        ),
        out_specs=(
            P(("dp", "col"), "row"),
            P(("dp", "col"), "row"),
            P("row"),
            P("row", None, "col"),
            P("row", None),
            P("row", "col"),
            P("col", "row"),
            P(None, "col"),
            P("col"),
            P(),
            P(),
            P("col"),
            P("col"),
            P("col"),
            P("col"),
        ),
        check_vma=False,
    )
```

profile of v0, /device:TPU:0, one launch (start us, length us, event | category | flops | bytes accessed | tf_op | source)
XLA Modules:
  0.0 1751.1 jit_solution(5665702625245222019)
XLA Ops:
  7.2 1.7 multiply_reduce_fusion.11
  9.6 2.1 fusion.53
  12.8 26.0 %fusion.116 = (bf16[1280,1,2560]{2,1,0:T(2,128)(2,1)S(1)}, bf16[1280,1,2560]{2,1,0:T(2,128)(2,1)}) fusion(bf16[1280,2,2560]{2,1,0:T(2,128)(2,1)} %param.22), kind=kLoop, calls=%fused_computation.231 | loop fusion | bytes 26214400 | tf_op jit(solution)/shard_map/slice | solution.py:172
  38.8 13.5 copy_bitcast_fusion
  52.3 18.4 %fusion.41 = f32[512,5416]{1,0:T(8,128)} fusion(bf16[512,1280]{1,0:T(8,128)(2,1)} %all-gather.5.cloned.1.call-done, bf16[1280,40]{1,0:T(8,128)(2,1)S(1)} %copy.146, bf16[1280,256]{1,0:T(8,128)(2,1)S(1)} %copy-done.88, bf16[1280,2560]{1,0:T(8,128)(2,1)} %get-tuple-element.342, bf16[1280,2560]{1,0:T(8,128)(2,1)} %get-tuple-element.343), kind=kOutput, calls=%fused_computation.76 | convolution fusion | flops 7154319360 | bytes 26267648 | tf_op jit(solution)/shard_map/dot_general | solution.py:175
  71.0 9.5 fusion.121
  84.6 9.0 reduce-scatter.5.cloned.1.call-done
  96.1 2.1 slice.225
  98.2 2.9 slice.224
  102.6 4.3 fusion.39
  106.9 2.5 copy.149
  109.4 1.4 slice.231
  113.7 1.9 fusion.76
  116.1 11.7 fusion.5
  127.8 4.3 fusion.33
  132.1 2.1 copy.153
  134.2 4.0 multiply_reduce_fusion.10
  138.2 4.9 psum.77
  144.2 3.9 multiply_reduce_fusion.3
  148.1 4.9 psum.78
  153.0 5.8 fusion.65
  158.8 3.4 copy.154
  166.0 1.2 copy-done.2
  167.2 2.3 multiply_reduce_fusion.8
  170.0 7.2 multiply_reduce_fusion.2
  177.2 15.9 fusion.12
  195.2 2.7 reduce-window.44
  198.8 6.1 fusion.69
  205.0 11.7 bitcast_add_fusion
  216.7 3.3 copy.172
  220.1 6.9 multiply_reduce_fusion.7
  227.0 4.0 multiply_reduce_fusion.6
  231.1 6.1 fusion.66
  237.8 1.5 convolution_add_fusion.1
  239.4 1.4 multiply_reduce_fusion.16
  240.8 1.6 multiply_reduce_fusion.15
  242.4 1.5 copy.165
  247.0 1.2 slice_multiply_fusion.1
  248.7 1.3 copy-done.13
  252.0 1.3 multiply_reduce_fusion.4
  253.7 1.7 add_convert_fusion
  257.2 15.5 all-gather.11.cloned.1.call-done
  272.7 17.6 %fusion.122 = f32[1280,5416]{0,1:T(8,128)} fusion(bf16[512,1280]{1,0:T(8,128)(2,1)S(1)} %copy-done.87, bf16[512,5416]{1,0:T(8,128)(2,1)} %all-gather.11.cloned.1.call-done), kind=kOutput, calls=%fused_computation.237 | convolution fusion | flops 7098859520 | bytes 34586624 | tf_op jit(solution)/shard_map/dot_general | solution.py:252
  290.3 1.3 slice-done.4
  292.0 1.7 broadcast_multiply_fusion
  293.9 15.0 fusion.40
  309.0 8.9 fusion.120
  318.1 1.5 copy-done.86
  319.6 8.0 fusion.123
  327.6 1.6 slice.242
  329.2 14.7 slice_bitcast_fusion.1
  343.9 14.5 pad_maximum_fusion
  359.3 72.7 %all-reduce.36.cloned.1.call-done = (f32[2,1280,256]{2,1,0:T(8,128)}, f32[6,2,2560]{2,0,1:T(8,128)}) async-done(((f32[2,1280,256]{2,1,0:T(8,128)}, f32[6,2,2560]{2,0,1:T(8,128)}), (f32[2,1280,256]{2,1,0:T(8,128)}, f32[6,2,2560]{2,0,1:T(8,128)})) %all-reduce.36.cloned.1.call-update) | async-done | bytes 2744336 | tf_op jit(solution)/shard_map/psum | solution.py:280
  432.0 1.6 dynamic-slice_reduce_fusion
  433.6 2.5 dynamic-slice_bitcast_fusion
  436.0 1.5 dynamic-slice_bitcast_fusion.1
  437.5 34.1 %reduce-scatter.11.cloned.1.call-done = f32[256,1280]{1,0:T(8,128)} async-done(((f32[512,1280]{1,0:T(8,128)}), f32[256,1280]{1,0:T(8,128)}) %reduce-scatter.11.cloned.1.call-update) | async-done | bytes 1310736 | tf_op jit(solution)/shard_map/reduce_scatter | solution.py:244
  471.7 1.9 fusion.58
  473.6 40.0 %all-reduce.30 = (f32[2,1280]{1,0:T(2,128)S(1)}, f32[5,256]{1,0:T(8,128)S(1)}, f32[3,2,40]{2,1,0:T(2,128)S(1)}) all-reduce(f32[2,1280]{1,0:T(2,128)S(1)} %broadcast_multiply_fusion.9, f32[5,256]{1,0:T(8,128)S(1)} %pad_maximum_fusion.5, ...), channel_id=1, replica_groups=mesh['dp'=8,'row'=2,'col'=2] {'dp','row','col'}, use_global_device_ids=true, to_apply=%region_28.29 | all-reduce | flops 4080 | bytes 32640 | tf_op jit(solution)/shard_map/psum | solution.py:280
  515.5 2.4 psum.79
  518.4 3.1 fusion.57
  521.5 1172.5 %all-reduce.38.cloned.1.call-done = (f32[1280,2,2560]{0,2,1:T(8,128)}, f32[1280,40]{0,1:T(8,128)}, f32[2560,1280]{1,0:T(8,128)}) async-done(((f32[1280,2,2560]{0,2,1:T(8,128)}, f32[1280,40]{0,1:T(8,128)}, f32[2560,1280]{1,0:T(8,128)}), (f32[1280,2,2560]{0,2,1:T(8,128)}, f32[1280,40]{0,1:T(8,128)}, f32[2560,1280]{1,0:T(8,128)})) %all-reduce.38.cloned.1.call-update) | async-done | bytes 39526416 | tf_op jit(solution)/shard_map/psum | solution.py:266
  1694.1 38.8 %copy.176 = f32[1280,2,2560]{2,1,0:T(2,128)} copy(f32[1280,2,2560]{0,2,1:T(8,128)} %get-tuple-element.270) | data formatting | bytes 52428800
  1733.5 10.5 copy.205
  (316 shorter events, 32.8 us)
Async XLA Ops:
  7.2 5.4 copy-start.44
  7.2 45.1 %all-gather.5.cloned.1.call-start = ((), (), s32[]{:S(2)}) async-start(), calls=%async_computation.4 | async-start | bytes 1966080 | tf_op jit(solution)/shard_map/all_gather | solution.py:171
  11.8 59.2 %all-gather.9.cloned.1.call-start = ((), (), s32[]{:S(2)}) async-start(), calls=%async_computation.8 | async-start | bytes 1966080 | tf_op jit(solution)/shard_map/all_gather | solution.py:222
  12.6 81.0 %reduce-scatter.5.cloned.1.call-start = ((), (), s32[]{:S(2)}) async-start(), calls=%async_computation.5 | async-start | bytes 16908288 | tf_op jit(solution)/shard_map/reduce_scatter | solution.py:174
  12.8 39.5 %copy-start.29 = (bf16[1280,40]{1,0:T(8,128)(2,1)}, bf16[1280,40]{1,0:T(8,128)(2,1)S(1)}, u32[]{:S(2)}) copy-start(bf16[1280,40]{1,0:T(8,128)(2,1)S(1)} %copy.146) | copy-start | bytes 307204
  38.8 13.5 copy-start.88
  70.8 73.4 %reduce-scatter.9.cloned.1.call-start = ((), (), s32[]{:S(2)}) async-start(), calls=%async_computation.9 | async-start | bytes 7864320 | tf_op jit(solution)/shard_map/reduce_scatter | solution.py:224
  80.6 13.0 copy-start.77
  80.6 192.1 %all-gather.11.cloned.1.call-start = ((), (), s32[]{:S(2)}) async-start(), calls=%async_computation.10 | async-start | bytes 8454144 | tf_op jit(solution)/shard_map/all_gather | solution.py:242
  82.5 19.0 %copy-start.37 = (f32[2560]{0:T(1024)}, f32[2560]{0:T(1024)S(1)}, u32[]{:S(2)}) copy-start(f32[2560]{0:T(1024)S(1)} %get-tuple-element.261) | copy-start | bytes 30724
  82.5 19.0 %copy-start.39 = (f32[2560]{0:T(1024)}, f32[2560]{0:T(1024)S(1)}, u32[]{:S(2)}) copy-start(f32[2560]{0:T(1024)S(1)} %get-tuple-element.263) | copy-start | bytes 30724
  82.5 19.0 %copy-start.41 = (f32[2560]{0:T(1024)}, f32[2560]{0:T(1024)S(1)}, u32[]{:S(2)}) copy-start(f32[2560]{0:T(1024)S(1)} %get-tuple-element.262) | copy-start | bytes 30724
  82.5 19.0 %copy-start.43 = (f32[2560]{0:T(1024)}, f32[2560]{0:T(1024)S(1)}, u32[]{:S(2)}) copy-start(f32[2560]{0:T(1024)S(1)} %get-tuple-element.264) | copy-start | bytes 30724
  82.5 12.0 copy-start.79
  82.6 15.6 copy-start.71
  82.6 45.1 %copy-start.52 = (f32[256]{0:T(256)}, f32[256]{0:T(256)S(1)}, u32[]{:S(2)}) copy-start(f32[256]{0:T(256)S(1)} %get-tuple-element.124) | copy-start | bytes 3076
  83.2 18.3 %copy-start.56 = (f32[256]{0:T(256)}, f32[256]{0:T(256)S(1)}, u32[]{:S(2)}) copy-start(f32[256]{0:T(256)S(1)} %get-tuple-element.335) | copy-start | bytes 3076
  83.2 18.3 %copy-start.59 = (f32[256]{0:T(256)}, f32[256]{0:T(256)S(1)}, u32[]{:S(2)}) copy-start(f32[256]{0:T(256)S(1)} %get-tuple-element.336) | copy-start | bytes 3076
  83.2 30.5 %copy-start.54 = (f32[256]{0:T(256)}, f32[256]{0:T(256)S(1)}, u32[]{:S(2)}) copy-start(f32[256]{0:T(256)S(1)} %get-tuple-element.334) | copy-start | bytes 3076
  95.4 17.4 copy-start.66
  95.4 5.7 slice-start
  96.1 5.0 slice-start.1
  101.5 5.4 copy-start.9
  109.4 18.4 %copy-start = (f32[256,2560]{0,1:T(8,128)}, f32[256,2560]{0,1:T(8,128)S(1)}, u32[]{:S(2)}) copy-start(f32[256,2560]{0,1:T(8,128)S(1)} %copy.149) | copy-start | bytes 7864324
  109.4 6.2 copy-start.72
  109.4 6.6 copy-start.45
  109.4 6.6 copy-start.51
  110.8 5.2 copy-start.21
  112.8 14.9 copy-start.19
  115.6 12.1 copy-start.23
  116.0 11.7 copy-start.83
  158.8 6.1 copy-start.33
  165.1 72.1 %copy-start.24 = (pred[256,256]{1,0:T(8,128)(4,1)}, pred[256,256]{1,0:T(8,128)(4,1)S(1)}, u32[]{:S(2)}) copy-start(pred[256,256]{1,0:T(8,128)(4,1)S(1)} %and_and_fusion) | copy-start | bytes 196612
  165.1 29.8 %copy-start.61 = (f32[1,256]{1,0:T(1,128)}, f32[1,256]{1,0:T(1,128)S(1)}, u32[]{:S(2)}) copy-start(f32[1,256]{1,0:T(1,128)S(1)} %slice_convert_fusion) | copy-start | bytes 3076
  169.9 7.3 copy-start.31
  169.9 7.2 copy-start.1
  170.0 7.2 copy-start.3
  193.1 44.2 %copy-start.26 = (f32[256,256]{1,0:T(8,128)}, f32[256,256]{1,0:T(8,128)S(1)}, u32[]{:S(2)}) copy-start(f32[256,256]{1,0:T(8,128)S(1)} %get-tuple-element.248) | copy-start | bytes 786436
  194.8 10.1 copy-start.68
  195.1 9.8 copy-start.32
  195.1 9.8 copy-start.84
  198.8 6.2 copy-start.4
  220.0 6.9 copy-start.8
  220.0 6.9 copy-start.10
  220.1 6.9 copy-start.55
  220.1 6.9 copy-start.57
  231.1 8.3 copy-start.22
  231.1 8.3 copy-start.25
  231.1 9.7 copy-start.20
  231.1 9.7 copy-start.58
  237.8 9.2 copy-start.15
  240.8 7.5 copy-start.42
  255.4 17.2 copy-start.87
  255.5 53.5 %all-gather.7.cloned.1.call-start = ((), (), s32[]{:S(2)}) async-start(), calls=%async_computation.6 | async-start | bytes 3932160 | tf_op jit(solution)/shard_map/all_gather | solution.py:213
  256.3 175.7 %all-reduce.36.cloned.1.call-start = ((), (), s32[]{:S(2)}) async-start(), calls=%async_computation.12 | async-start | bytes 5570560 | tf_op jit(solution)/shard_map/psum | solution.py:280
  293.8 177.8 %reduce-scatter.11.cloned.1.call-start = ((), (), s32[]{:S(2)}) async-start(), calls=%async_computation.11 | async-start | bytes 3932160 | tf_op jit(solution)/shard_map/reduce_scatter | solution.py:244
  308.9 209.5 %reduce-scatter.7.cloned.1.call-start = ((), (), s32[]{:S(2)}) async-start(), calls=%async_computation.7 | async-start | bytes 3932160 | tf_op jit(solution)/shard_map/reduce_scatter | solution.py:215
  317.9 1376.2 %all-reduce.38.cloned.1.call-start = ((), (), s32[]{:S(2)}) async-start(), calls=%async_computation.13 | async-start | bytes 79052800 | tf_op jit(solution)/shard_map/psum | solution.py:266
  358.5 113.2 %copy-start.16 = (bf16[256,2560]{1,0:T(8,128)(2,1)S(1)}, bf16[256,2560]{1,0:T(8,128)(2,1)}, u32[]{:S(2)}) copy-start(bf16[256,2560]{1,0:T(8,128)(2,1)} %param.17) | copy-start | bytes 3932164
  358.5 113.2 %copy-start.36 = (f32[1280]{0:T(1024)S(1)}, f32[1280]{0:T(1024)}, u32[]{:S(2)}) copy-start(f32[1280]{0:T(1024)} %copy-done.35) | copy-start | bytes 15364
  358.5 113.2 %copy-start.64 = (f32[256]{0:T(256)S(1)}, f32[256]{0:T(256)}, u32[]{:S(2)}) copy-start(f32[256]{0:T(256)} %copy-done.63) | copy-start | bytes 3076
  358.5 159.9 %copy-start.18 = (bf16[256,1280]{1,0:T(8,128)(2,1)S(1)}, bf16[256,1280]{1,0:T(8,128)(2,1)}, u32[]{:S(2)}) copy-start(bf16[256,1280]{1,0:T(8,128)(2,1)} %param.18) | copy-start | bytes 1966084
  471.7 46.8 %copy-start.17 = (f32[256,1280]{1,0:T(8,128)S(1)}, f32[256,1280]{1,0:T(8,128)}, u32[]{:S(2)}) copy-start(f32[256,1280]{1,0:T(8,128)} %reduce-scatter.11.cloned.1.call-done) | copy-start | bytes 3932164
  1694.0 38.8 %copy-start.34 = (f32[1280,40]{0,1:T(8,128)S(1)}, f32[1280,40]{0,1:T(8,128)}, u32[]{:S(2)}) copy-start(f32[1280,40]{0,1:T(8,128)} %get-tuple-element.349) | copy-start | bytes 614404
  (43 other events, 71.7 us)
Sparse Core Ops, SparseCore 0:
  11.9 26.9 all-gather.4
  40.4 24.2 all-gather.8
  70.9 22.6 reduce-scatter.4
  95.7 14.4 reduce-scatter.8
  255.6 17.0 all-gather.10
  274.7 12.5 all-gather.6
  294.3 137.5 all-reduce.35
  434.3 37.3 reduce-scatter.10
  473.9 38.2 reduce-scatter.6
  518.2 1175.8 all-reduce.37
where the time goes:
time: 1760 us; the launch traced here: 1750 us
  waiting for transfers between devices  1300 us (74%)
  local copies, waits for them, and re-layouts  152 us (9%)
  matrix products  146 us (8%)
  other arithmetic  78.7 us (4%)
  blocking collectives  52.3 us (3%)
    psum x1, waiting for transfers between devices, per_device(): lax.psum((inproj_part, steps_part, outproj_total), 'dp')  1170 us
    psum x1, waiting for transfers between devices, per_device(): lax.psum((gain_slot, shared_slot, head_slot, chan_slot, shared_stack), ('...  72.7 us
    unnamed x196, local copies, waits for them, and re-layouts  59.1 us
    psum x1, blocking collectives, per_device(): lax.psum((gain_slot, shared_slot, head_slot, chan_slot, shared_stack), ('...  40 us
    dot_general x3, matrix products, one_block(): within = jnp.einsum('tsh,shp->thp', weights, vals, precision=PRECISE)  39.3 us
  transfers between devices with their start and end apart: 10, of which 5 were waited for; matrix products, arithmetic and copies ran while one was open for 12% of the time, Pallas kernels for 0%

commit v1 on v0

--- a/solution.py
+++ b/solution.py
@@ -278,7 +278,7 @@
     chan_slot = col_hot[None, :, None] * chan_stack[:, None, :]
     shared_stack = jnp.concatenate([local_grads[3], local_grads[4][None, :]], axis=0)
     summed = lax.psum(
-        (gain_slot, shared_slot, head_slot, chan_slot, shared_stack), ("dp", "row", "col")
+        lax.psum((gain_slot, shared_slot, head_slot, chan_slot, shared_stack), ("row", "col")), "dp"
     )
     gain_total = lax.dynamic_index_in_dim(summed[0], row_index, 0, keepdims=False)
     shared_total = lax.dynamic_index_in_dim(summed[1], row_index, 0, keepdims=False)

time: 1760 us -> 1780 us (1.011)
    psum x1, waiting for transfers between devices: 1170 us -> 1250 us  [per_device(): lax.psum((inproj_part, steps_part, outproj_total), 'dp')]
    psum x1, waiting for transfers between devices: 72.7 us -> 0.01 us  [per_device(): lax.psum((gain_slot, shared_slot, head_slot, chan_slot, shared_stack), ('...]
    psum x0 -> x1, blocking collectives: none -> 37.1 us  [per_device(): lax.psum(lax.psum((gain_slot, shared_slot, head_slot, chan_slot, shared_s...]
    psum x1, blocking collectives: 40 us -> 12 us  [per_device(): lax.psum((gain_slot, shared_slot, head_slot, chan_slot, shared_stack), ('...]
    unnamed x196 -> x198, local copies, waits for them, and re-layouts: 59.1 us -> 59.2 us
  transfers between devices with their start and end apart: 10 -> 10, of which waited for: 5 -> 4; matrix products, arithmetic and copies ran while one was open for 12% -> 12% of each run, Pallas kernels for 0% -> 0%
where the time goes in v1:
time: 1780 us; the launch traced here: 1770 us
  waiting for transfers between devices  1310 us (74%)
  local copies, waits for them, and re-layouts  151 us (8%)
  matrix products  145 us (8%)
  other arithmetic  78.7 us (4%)
  blocking collectives  61.4 us (3%)
    psum x1, waiting for transfers between devices, per_device(): lax.psum((inproj_part, steps_part, outproj_total), 'dp')  1250 us
    unnamed x198, local copies, waits for them, and re-layouts  59.2 us
    dot_general x3, matrix products, one_block(): within = jnp.einsum('tsh,shp->thp', weights, vals, precision=PRECISE)  39.3 us
    reduce_scatter x1, waiting for transfers between devices, per_device(): lax.psum_scatter(lax.dot_general(row_piece, weight_in, (((1,), (1,)), (()...  38.2 us
    psum x1, blocking collectives, per_device(): lax.psum(lax.psum((gain_slot, shared_slot, head_slot, chan_slot, shared_s...  37.1 us
  transfers between devices with their start and end apart: 10, of which 4 were waited for; matrix products, arithmetic and copies ran while one was open for 12% of the time, Pallas kernels for 0%

profile of v1, /device:TPU:0, one launch (start us, length us, event | category | flops | bytes accessed | tf_op | source)
XLA Modules:
  0.0 1768.5 jit_solution(12388100788643615600)
XLA Ops:
  7.2 1.7 multiply_reduce_fusion.11
  9.6 2.1 fusion.53
  12.8 26.0 %fusion.116 = (bf16[1280,1,2560]{2,1,0:T(2,128)(2,1)S(1)}, bf16[1280,1,2560]{2,1,0:T(2,128)(2,1)}) fusion(bf16[1280,2,2560]{2,1,0:T(2,128)(2,1)} %param.22), kind=kLoop, calls=%fused_computation.231 | loop fusion | bytes 26214400 | tf_op jit(solution)/shard_map/slice | solution.py:172
  38.8 13.5 copy_bitcast_fusion
  52.3 18.4 %fusion.41 = f32[512,5416]{1,0:T(8,128)} fusion(bf16[512,1280]{1,0:T(8,128)(2,1)} %all-gather.5.cloned.1.call-done, bf16[1280,40]{1,0:T(8,128)(2,1)S(1)} %copy.146, bf16[1280,256]{1,0:T(8,128)(2,1)S(1)} %copy-done.89, bf16[1280,2560]{1,0:T(8,128)(2,1)} %get-tuple-element.347, bf16[1280,2560]{1,0:T(8,128)(2,1)} %get-tuple-element.348), kind=kOutput, calls=%fused_computation.76 | convolution fusion | flops 7154319360 | bytes 26267648 | tf_op jit(solution)/shard_map/dot_general | solution.py:175
  71.0 9.5 fusion.121
  84.6 9.0 reduce-scatter.5.cloned.1.call-done
  96.1 2.1 slice.225
  98.2 2.9 slice.224
  102.6 4.3 fusion.39
  106.9 2.5 copy.149
  109.4 1.4 slice.231
  113.7 1.9 fusion.76
  116.1 11.7 fusion.5
  127.8 4.3 fusion.33
  132.1 2.1 copy.153
  134.2 4.0 multiply_reduce_fusion.10
  138.2 4.9 psum.112
  144.2 3.9 multiply_reduce_fusion.3
  148.1 4.9 psum.113
  153.0 5.8 fusion.65
  158.8 3.4 copy.154
  166.0 1.2 copy-done.2
  167.2 2.3 multiply_reduce_fusion.8
  170.0 7.2 multiply_reduce_fusion.2
  177.2 15.9 fusion.12
  195.2 2.7 reduce-window.44
  198.8 6.1 fusion.69
  205.0 11.7 bitcast_add_fusion
  216.7 3.3 copy.172
  220.1 6.9 multiply_reduce_fusion.7
  227.0 4.0 multiply_reduce_fusion.6
  231.1 6.1 fusion.66
  237.8 1.5 convolution_add_fusion.1
  239.4 1.4 multiply_reduce_fusion.16
  240.8 1.6 multiply_reduce_fusion.15
  242.4 1.5 copy.165
  247.0 1.2 slice_multiply_fusion.1
  248.7 1.3 copy-done.13
  252.0 1.3 multiply_reduce_fusion.4
  253.7 1.7 add_convert_fusion
  257.2 15.5 all-gather.11.cloned.1.call-done
  272.7 17.6 fusion.122
  290.3 1.3 slice-done.4
  292.0 1.7 broadcast_multiply_fusion
  293.9 15.0 fusion.40
  309.0 8.8 fusion.120
  318.0 1.5 copy-done.87
  319.5 8.0 fusion.123
  327.5 1.6 slice.242
  329.1 15.2 slice_bitcast_fusion.1
  344.3 14.5 pad_maximum_fusion
  359.6 38.2 %reduce-scatter.11.cloned.1.call-done = f32[256,1280]{1,0:T(8,128)} async-done(((f32[512,1280]{1,0:T(8,128)}), f32[256,1280]{1,0:T(8,128)}) %reduce-scatter.11.cloned.1.call-update) | async-done | bytes 1310736 | tf_op jit(solution)/shard_map/reduce_scatter | solution.py:244
  397.8 1.9 fusion.58
  399.8 12.0 all-reduce.32
  411.8 37.1 %all-reduce.30 = (f32[2,1280]{1,0:T(2,128)S(1)}, f32[5,256]{1,0:T(8,128)S(1)}, f32[3,2,40]{2,1,0:T(2,128)S(1)}) all-reduce(f32[2,1280]{1,0:T(2,128)S(1)} %get-tuple-element.273, f32[5,256]{1,0:T(8,128)S(1)} %get-tuple-element.274, f32[3,2,40]{2,1,0:T(2,128)S(1)} %get-tuple-element.275), channel_id=1, replica_groups=mesh['dp'=8,'row'=2,'col'=2] {'dp'}, use_global_device_ids=true, to_apply=%region_29.30 | all-reduce | flops 4080 | bytes 32640 | tf_op jit(solution)/shard_map/psum | solution.py:280
  450.7 2.4 psum.114
  453.7 3.1 fusion.57
  456.7 1250.3 %all-reduce.37.cloned.1.call-done = (f32[1280,2,2560]{0,2,1:T(8,128)}, f32[2,1280,256]{2,1,0:T(8,128)}, f32[1280,40]{0,1:T(8,128)}, f32[2560,1280]{1,0:T(8,128)}, f32[6,2,2560]{2,0,1:T(8,128)}) async-done(((f32[1280,2,2560]{0,2,1:T(8,128)}, f32[2,1280,256]{2,1,0:T(8,128)}, f32[1280,40]{0,1:T(8,128)}, f32[2560,1280]{1,0:T(8,128)}, f32[6,2,2560]{2,0,1:T(8,128)}), (f32[1280,2,2560]{0,2,1:T(8,128)}, ...) | async-done | bytes 42270736 | tf_op jit(solution)/shard_map/psum | solution.py:266
  1707.1 38.9 %copy.176 = f32[1280,2,2560]{2,1,0:T(2,128)} copy(f32[1280,2,2560]{0,2,1:T(8,128)} %get-tuple-element.268) | data formatting | bytes 52428800
  1746.0 1.6 dynamic-slice_bitcast_fusion.1
  1747.5 1.1 dynamic-slice_bitcast_fusion
  1748.7 1.6 dynamic-slice_reduce_fusion
  1751.0 10.5 copy.207
  (319 shorter events, 32.8 us)
Async XLA Ops:
  7.2 5.4 copy-start.45
  7.2 45.1 %all-gather.5.cloned.1.call-start = ((), (), s32[]{:S(2)}) async-start(), calls=%async_computation.4 | async-start | bytes 1966080 | tf_op jit(solution)/shard_map/all_gather | solution.py:171
  11.8 59.2 %all-gather.9.cloned.1.call-start = ((), (), s32[]{:S(2)}) async-start(), calls=%async_computation.8 | async-start | bytes 1966080 | tf_op jit(solution)/shard_map/all_gather | solution.py:222
  12.6 81.0 %reduce-scatter.5.cloned.1.call-start = ((), (), s32[]{:S(2)}) async-start(), calls=%async_computation.5 | async-start | bytes 16908288 | tf_op jit(solution)/shard_map/reduce_scatter | solution.py:174
  12.8 39.5 %copy-start.30 = (bf16[1280,40]{1,0:T(8,128)(2,1)}, bf16[1280,40]{1,0:T(8,128)(2,1)S(1)}, u32[]{:S(2)}) copy-start(bf16[1280,40]{1,0:T(8,128)(2,1)S(1)} %copy.146) | copy-start | bytes 307204
  38.8 13.5 copy-start.89
  70.8 73.4 %reduce-scatter.9.cloned.1.call-start = ((), (), s32[]{:S(2)}) async-start(), calls=%async_computation.9 | async-start | bytes 7864320 | tf_op jit(solution)/shard_map/reduce_scatter | solution.py:224
  80.6 13.0 copy-start.78
  80.6 192.1 %all-gather.11.cloned.1.call-start = ((), (), s32[]{:S(2)}) async-start(), calls=%async_computation.10 | async-start | bytes 8454144 | tf_op jit(solution)/shard_map/all_gather | solution.py:242
  82.5 19.0 %copy-start.38 = (f32[2560]{0:T(1024)}, f32[2560]{0:T(1024)S(1)}, u32[]{:S(2)}) copy-start(f32[2560]{0:T(1024)S(1)} %get-tuple-element.261) | copy-start | bytes 30724
  82.5 19.0 %copy-start.40 = (f32[2560]{0:T(1024)}, f32[2560]{0:T(1024)S(1)}, u32[]{:S(2)}) copy-start(f32[2560]{0:T(1024)S(1)} %get-tuple-element.263) | copy-start | bytes 30724
  82.5 19.0 %copy-start.42 = (f32[2560]{0:T(1024)}, f32[2560]{0:T(1024)S(1)}, u32[]{:S(2)}) copy-start(f32[2560]{0:T(1024)S(1)} %get-tuple-element.262) | copy-start | bytes 30724
  82.5 19.0 %copy-start.44 = (f32[2560]{0:T(1024)}, f32[2560]{0:T(1024)S(1)}, u32[]{:S(2)}) copy-start(f32[2560]{0:T(1024)S(1)} %get-tuple-element.264) | copy-start | bytes 30724
  82.5 12.0 copy-start.80
  82.6 15.6 copy-start.72
  82.6 45.1 %copy-start.53 = (f32[256]{0:T(256)}, f32[256]{0:T(256)S(1)}, u32[]{:S(2)}) copy-start(f32[256]{0:T(256)S(1)} %get-tuple-element.124) | copy-start | bytes 3076
  83.2 18.3 %copy-start.57 = (f32[256]{0:T(256)}, f32[256]{0:T(256)S(1)}, u32[]{:S(2)}) copy-start(f32[256]{0:T(256)S(1)} %get-tuple-element.340) | copy-start | bytes 3076
  83.2 18.3 %copy-start.60 = (f32[256]{0:T(256)}, f32[256]{0:T(256)S(1)}, u32[]{:S(2)}) copy-start(f32[256]{0:T(256)S(1)} %get-tuple-element.341) | copy-start | bytes 3076
  83.2 30.5 %copy-start.55 = (f32[256]{0:T(256)}, f32[256]{0:T(256)S(1)}, u32[]{:S(2)}) copy-start(f32[256]{0:T(256)S(1)} %get-tuple-element.339) | copy-start | bytes 3076
  95.4 17.4 copy-start.67
  95.4 5.7 slice-start
  96.1 5.0 slice-start.1
  101.5 5.4 copy-start.9
  109.4 18.4 %copy-start = (f32[256,2560]{0,1:T(8,128)}, f32[256,2560]{0,1:T(8,128)S(1)}, u32[]{:S(2)}) copy-start(f32[256,2560]{0,1:T(8,128)S(1)} %copy.149) | copy-start | bytes 7864324
  109.4 6.2 copy-start.73
  109.4 6.6 copy-start.46
  109.4 6.6 copy-start.52
  110.8 5.2 copy-start.21
  112.8 14.9 copy-start.19
  115.6 12.1 copy-start.23
  116.0 11.7 copy-start.84
  158.8 6.1 copy-start.34
  165.1 72.1 %copy-start.24 = (pred[256,256]{1,0:T(8,128)(4,1)}, pred[256,256]{1,0:T(8,128)(4,1)S(1)}, u32[]{:S(2)}) copy-start(pred[256,256]{1,0:T(8,128)(4,1)S(1)} %and_and_fusion) | copy-start | bytes 196612
  165.1 29.8 %copy-start.62 = (f32[1,256]{1,0:T(1,128)}, f32[1,256]{1,0:T(1,128)S(1)}, u32[]{:S(2)}) copy-start(f32[1,256]{1,0:T(1,128)S(1)} %slice_convert_fusion) | copy-start | bytes 3076
  169.9 7.3 copy-start.32
  169.9 7.2 copy-start.1
  170.0 7.2 copy-start.3
  193.1 44.1 %copy-start.26 = (f32[256,256]{1,0:T(8,128)}, f32[256,256]{1,0:T(8,128)S(1)}, u32[]{:S(2)}) copy-start(f32[256,256]{1,0:T(8,128)S(1)} %get-tuple-element.248) | copy-start | bytes 786436
  194.8 10.1 copy-start.69
  195.1 9.8 copy-start.33
  195.1 9.8 copy-start.85
  198.8 6.2 copy-start.4
  220.0 6.9 copy-start.8
  220.0 6.9 copy-start.10
  220.0 6.9 copy-start.56
  220.1 6.9 copy-start.58
  231.1 8.3 copy-start.22
  231.1 8.3 copy-start.25
  231.1 9.7 copy-start.20
  231.1 9.7 copy-start.59
  237.8 9.2 copy-start.15
  240.8 7.5 copy-start.43
  255.4 17.2 copy-start.88
  255.5 53.5 %all-gather.7.cloned.1.call-start = ((), (), s32[]{:S(2)}) async-start(), calls=%async_computation.6 | async-start | bytes 3932160 | tf_op jit(solution)/shard_map/all_gather | solution.py:213
  256.3 102.5 %all-reduce.39.cloned.1.call-start = ((), (), s32[]{:S(2)}) async-start(), calls=%async_computation.13 | async-start | bytes 5570560 | tf_op jit(solution)/shard_map/psum | solution.py:281
  293.8 104.0 %reduce-scatter.11.cloned.1.call-start = ((), (), s32[]{:S(2)}) async-start(), calls=%async_computation.11 | async-start | bytes 3932160 | tf_op jit(solution)/shard_map/reduce_scatter | solution.py:244
  308.9 144.8 %reduce-scatter.7.cloned.1.call-start = ((), (), s32[]{:S(2)}) async-start(), calls=%async_computation.7 | async-start | bytes 3932160 | tf_op jit(solution)/shard_map/reduce_scatter | solution.py:215
  317.8 1389.3 %all-reduce.37.cloned.1.call-start = ((), (), s32[]{:S(2)}) async-start(), calls=%async_computation.12 | async-start | bytes 84623360 | tf_op jit(solution)/shard_map/psum | solution.py:266
  358.8 39.0 %copy-start.16 = (bf16[256,2560]{1,0:T(8,128)(2,1)S(1)}, bf16[256,2560]{1,0:T(8,128)(2,1)}, u32[]{:S(2)}) copy-start(bf16[256,2560]{1,0:T(8,128)(2,1)} %param.17) | copy-start | bytes 3932164
  358.8 39.0 %copy-start.37 = (f32[1280]{0:T(1024)S(1)}, f32[1280]{0:T(1024)}, u32[]{:S(2)}) copy-start(f32[1280]{0:T(1024)} %copy-done.36) | copy-start | bytes 15364
  358.8 39.0 %copy-start.65 = (f32[256]{0:T(256)S(1)}, f32[256]{0:T(256)}, u32[]{:S(2)}) copy-start(f32[256]{0:T(256)} %copy-done.64) | copy-start | bytes 3076
  358.9 94.8 %copy-start.18 = (bf16[256,1280]{1,0:T(8,128)(2,1)S(1)}, bf16[256,1280]{1,0:T(8,128)(2,1)}, u32[]{:S(2)}) copy-start(bf16[256,1280]{1,0:T(8,128)(2,1)} %param.18) | copy-start | bytes 1966084
  397.8 55.8 %copy-start.17 = (f32[256,1280]{1,0:T(8,128)S(1)}, f32[256,1280]{1,0:T(8,128)}, u32[]{:S(2)}) copy-start(f32[256,1280]{1,0:T(8,128)} %reduce-scatter.11.cloned.1.call-done) | copy-start | bytes 3932164
  1707.1 40.5 %copy-start.27 = (f32[2,1280,256]{2,1,0:T(8,128)S(1)}, f32[2,1280,256]{2,1,0:T(8,128)}, u32[]{:S(2)}) copy-start(f32[2,1280,256]{2,1,0:T(8,128)} %get-tuple-element.269) | copy-start | bytes 7864324
  (44 other events, 76.0 us)
Sparse Core Ops, SparseCore 0:
  11.9 26.9 all-gather.4
  40.4 24.2 all-gather.8
  70.9 22.6 reduce-scatter.4
  95.7 14.4 reduce-scatter.8
  255.6 17.0 all-gather.10
  274.7 12.5 all-gather.6
  293.9 63.9 all-reduce.38
  360.1 37.6 reduce-scatter.10
  400.1 38.0 reduce-scatter.6
  443.9 1263.0 all-reduce.36
